TPU v7x, 32 devices: a whole 2x2x4 slice. The times are simulated.
32 devices in a mesh: anim: 8 (over y, x, core), mark: 4 (over z).
Axes of the slice: x: 2, y: 2, z: 4, core: 2. Of those that a mesh axis runs over, the one named last changes fastest.
Arguments:
- solution: float32 [2, 65536], P(None, 'anim'), may hold values from -6 to 6
- residual: float32 [2, 65536], P(None, 'anim'), may hold values from -18 to 18
- direction: float32 [2, 65536], P(None, 'anim'), may hold values from -18 to 18
- record_inverse: float32 [3, 65536], P(None, 'anim'), may hold values from -1 to 2, as said below
- precondition: float32 [3, 65536], P(None, 'anim'), may hold values from -0.3 to 0.6, as said below
- genetic_inverse: float32 [2, 2], replicated, may hold values from -1 to 1.6, as said below
- sire_slot: int32 [65536], P('anim'), may hold values from -1 to 12287, as said below
- dam_slot: int32 [65536], P('anim'), may hold values from -1 to 12287, as said below
- send_rows: int32 [8, 8, 512], P('anim'), may hold values from -1 to 8191, as said below
- genotyped_row: int32 [8192], P('anim'), may hold values from 0 to 8191, as said below
- genotypes: int32 [8192, 8192], P('anim', 'mark'), may hold values from 0 to 2
- allele_freq: float32 [8192], P('mark'), may hold values from 0.05 to 0.5
- marker_weight: float32 [8192], P('mark'), may hold values from 0.2 to 5
Outputs:
- new_solution: float32 [2, 65536], P(None, 'anim')
- new_residual: float32 [2, 65536], P(None, 'anim')
- new_direction: float32 [2, 65536], P(None, 'anim')
Inputs may be any that keep to these rules, and one draw needn't show every extreme that they name: `sire_slot`: A slot below 0 marks an unknown parent, one from 0 to 8191 a row of the animal's own block, never the animal itself; a larger slot s names position (s - 8192) % 512 of the list that block (s - 8192) // 512 sends to the animal's block, and that position of send_rows is 0 or more. Every such used position is named by some animal of the receiving block. `dam_slot`: as for sire_slot. In each list send_rows[s, b, :] the used positions come first and hold distinct rows, the rest hold -1; a block's list to itself is empty; in every draw some block receives 512 used positions from every other block. `genotyped_row`: distinct within each block of 1024 genotype rows. `record_inverse`: each animal's triple (a, c, d) has a, d > 0 and |c| <= 0.5 sqrt(a d). `precondition`: each animal's triple (a, c, d) has a, d > 0 and |c| <= 0.5 sqrt(a d). `genetic_inverse`: Symmetric, diagonal entries positive, off-diagonal at most 0.6 times the root of their product in magnitude.
All inputs are finite; a program needn't handle non-finite values.
Results may differ from a plain program's by a relative error of at most 0.0001.
Values sent between devices are 32-bit elements; how exact they have to be, the bound alone decides.
A program may use at most 128 MiB of HBM per device.

v0:
```python
import jax
import jax.numpy as jnp
from jax import lax
from jax.sharding import PartitionSpec as P


def apply_block(triple, vector):
    upper_row = triple[0] * vector[0] + triple[1] * vector[1]
    lower_row = triple[1] * vector[0] + triple[2] * vector[1]
    return jnp.stack([upper_row, lower_row])


def genetic_apply(matrix, vector):
    upper_row = matrix[0, 0] * vector[0] + matrix[0, 1] * vector[1]
    lower_row = matrix[1, 0] * vector[0] + matrix[1, 1] * vector[1]
    return jnp.stack([upper_row, lower_row])


def pedigree_apply(direction, sire_slot, dam_slot, send_rows):
    animals = direction.shape[1]
    owned_rows = send_rows[0]
    sources, capacity = owned_rows.shape
    slot_total = sources * capacity
    outgoing = jnp.where(owned_rows[None] >= 0, direction[:, jnp.maximum(owned_rows, 0)], 0.0)
    ghosts = lax.all_to_all(outgoing, "anim", split_axis=1, concat_axis=1, tiled=True)
    lookup_table = jnp.concatenate(
        [direction, ghosts.reshape(2, slot_total), jnp.zeros((2, 1), jnp.float32)], axis=1
    )
    sentinel = animals + slot_total
    sire_index = jnp.where(sire_slot < 0, sentinel, sire_slot)
    dam_index = jnp.where(dam_slot < 0, sentinel, dam_slot)
    known_count = (sire_slot >= 0).astype(jnp.float32) + (dam_slot >= 0).astype(jnp.float32)
    factor = 1.0 / (1.0 - 0.25 * known_count)
    sampling = factor * (
        direction - 0.5 * (lookup_table[:, sire_index] + lookup_table[:, dam_index])
    )
    spread = jnp.zeros((2, sentinel + 1), jnp.float32)
    spread = spread.at[:, sire_index].add(-0.5 * sampling)
    spread = spread.at[:, dam_index].add(-0.5 * sampling)
    outbound = spread[:, animals:sentinel].reshape(2, sources, capacity)
    inbound = lax.all_to_all(outbound, "anim", split_axis=1, concat_axis=1, tiled=True)
    target = jnp.where(owned_rows >= 0, owned_rows, animals)
    gathered_back = jnp.zeros((2, animals + 1), jnp.float32).at[:, target].add(inbound)
    return sampling + spread[:, :animals] + gathered_back[:, :animals]


def genomic_apply(direction, genotyped_row, genotypes, allele_freq, marker_weight):
    animals = direction.shape[1]
    picked = direction[:, genotyped_row]
    centered = genotypes.astype(jnp.float32) - 2.0 * allele_freq[None, :]
    partial_markers = jnp.dot(picked, centered, precision=lax.Precision.HIGHEST)
    marker_total = lax.psum(partial_markers, "anim")
    total_markers = centered.shape[1] * lax.axis_size("mark")
    scaled = marker_total * marker_weight[None, :] / total_markers
    partial_rows = lax.dot_general(
        scaled, centered, (((1,), (1,)), ((), ())), precision=lax.Precision.HIGHEST
    )
    genomic = lax.psum(partial_rows, "mark")
    return jnp.zeros((2, animals), jnp.float32).at[:, genotyped_row].add(genomic)


def on_device(
    solution,
    residual,
    direction,
    record_inverse,
    precondition,
    genetic_inverse,
    sire_slot,
    dam_slot,
    send_rows,
    genotyped_row,
    genotypes,
    allele_freq,
    marker_weight,
):
    pedigree_term = pedigree_apply(direction, sire_slot, dam_slot, send_rows)
    genomic_term = genomic_apply(direction, genotyped_row, genotypes, allele_freq, marker_weight)
    image = apply_block(record_inverse, direction) + genetic_apply(
        genetic_inverse, pedigree_term + genomic_term
    )
    scaled_residual = apply_block(precondition, residual)
    scaled_image = apply_block(precondition, image)
    old_product, curvature_sum, cross_term, image_term = lax.psum(
        (
            jnp.sum(residual * scaled_residual),
            jnp.sum(direction * image),
            jnp.sum(image * scaled_residual),
            jnp.sum(image * scaled_image),
        ),
        "anim",
    )
    step_size = old_product / curvature_sum
    new_solution = solution + step_size * direction
    new_residual = residual - step_size * image
    new_scaled = scaled_residual - step_size * scaled_image
    new_product = old_product - 2.0 * step_size * cross_term + step_size * step_size * image_term
    new_direction = new_scaled + new_product / old_product * direction
    return (new_solution, new_residual, new_direction)


def solution(mesh):
    return jax.shard_map(
        on_device,
        mesh=mesh,
        in_specs=(
            P(None, "anim"),
            P(None, "anim"),
            P(None, "anim"),
            P(None, "anim"),
            P(None, "anim"),
            P(),
            P("anim"),
            P("anim"),
            P("anim", None, None),
            P("anim"),
            P("anim", "mark"),
            P("mark"),
            P("mark"),
        ),
        out_specs=(P(None, "anim"), P(None, "anim"), P(None, "anim")),
        check_vma=False,
    )
```

profile of v0, /device:TPU:0, one launch (start us, length us, event | category | flops | bytes accessed | tf_op | source)
XLA Modules:
  0.0 347.9 jit_solution(14814706310013338081)
XLA Ops:
  2.2 3.3 copy.85
  5.6 13.0 %gather_fusion = f32[4096,2]{1,0:T(8,128)S(1)} fusion(f32[2,8192]{0,1:T(8,128)} %copy.85, s32[4096]{0:T(1024)S(1)} %broadcast_clamp_fusion.2), kind=kCustom, calls=%fused_computation | custom fusion | bytes 81920 | tf_op jit(solution)/shard_map/gather | solution.py:24
  19.8 5.2 %all-to-all-start = ((f32[2,8,512]{2,0,1:T(2,128)}), f32[2,8,512]{2,0,1:T(2,128)S(1)}, u32[]{:S(2)}, u32[]{:S(2)}) async-start(f32[2,8,512]{2,0,1:T(2,128)} %select_bitcast_fusion), calls=%async_computation | async-start | bytes 65536 | tf_op jit(solution)/shard_map/all_to_all | solution.py:25
  25.2 5.0 %gather_fusion.3 = f32[1024,2]{1,0:T(8,128)S(1)} fusion(f32[2,8192]{0,1:T(8,128)} %copy.85, s32[1024]{0:T(1024)S(1)} %get-tuple-element.36), kind=kCustom, calls=%fused_computation.3 | custom fusion | bytes 20480 | tf_op jit(solution)/shard_map/gather | solution.py:49
  30.2 6.8 %fusion.1 = f32[2,2048]{1,0:T(2,128)S(1)} fusion(f32[1024,2]{1,0:T(8,128)S(1)} %gather_fusion.3, s32[1024,2048]{1,0:T(8,128)} %param.23, f32[2048]{0:T(1024)S(1)} %broadcast_multiply_fusion), kind=kOutput, calls=%fused_computation.10 | convolution fusion | flops 54525952 | bytes 8421376 | tf_op jit(solution)/shard_map/dot_general | solution.py:51
  37.0 24.8 %psum.43 = f32[2,2048]{1,0:T(2,128)S(1)} all-reduce(f32[2,2048]{1,0:T(2,128)S(1)} %fusion.1), channel_id=1, replica_groups=mesh['anim'=8,'mark'=4] {'anim'}, use_global_device_ids=true, to_apply=%region_5.6 | all-reduce | flops 4096 | bytes 32768 | tf_op jit(solution)/shard_map/psum | solution.py:52
  61.9 9.1 %fusion = f32[2,1024]{1,0:T(2,128)S(1)} fusion(s32[1024,2048]{1,0:T(8,128)} %param.23, f32[2048]{0:T(1024)S(1)} %broadcast_multiply_fusion, f32[2,2048]{1,0:T(2,128)S(1)} %psum.43, f32[2048]{0:T(1024)S(1)} %copy-done.7), kind=kOutput, calls=%fused_computation.9 | convolution fusion | flops 54534144 | bytes 8429568 | tf_op jit(solution)/shard_map/dot_general | solution.py:55
  71.1 4.1 %copy.87 = f32[2,12289]{0,1:T(8,128)} copy(f32[2,12289]{1,0:T(2,128)S(1)} %maximum_maximum_fusion) | data formatting | bytes 196624 | tf_op jit(solution)/shard_map/concatenate | solution.py:26
  75.2 30.7 %gather_fusion.2 = f32[8192,2]{1,0:T(8,128)} fusion(f32[2,12289]{0,1:T(8,128)} %copy.87, s32[8192]{0:T(1024)S(1)} %get-tuple-element.31), kind=kCustom, calls=%fused_computation.2 | custom fusion | bytes 163840 | tf_op jit(solution)/shard_map/gather | solution.py:35
  105.9 2.8 copy.90
  108.7 30.7 %gather_fusion.1 = f32[8192,2]{1,0:T(8,128)} fusion(f32[2,12289]{0,1:T(8,128)} %copy.87, s32[8192]{0:T(1024)S(1)} %get-tuple-element.32), kind=kCustom, calls=%fused_computation.1 | custom fusion | bytes 163840 | tf_op jit(solution)/shard_map/gather | solution.py:35
  139.4 2.8 copy.89
  145.1 47.3 %scatter_custom_fusion = f32[2,12289]{0,1:T(8,128)} fusion(s32[8192]{0:T(1024)S(1)} %get-tuple-element.33, f32[8192,2]{1,0:T(8,128)} %copy.91, f32[]{:T(128)} %constant.12.clone.1), kind=kCustom, calls=%fused_computation.13 | custom fusion | flops 16384 | bytes 98824 | tf_op jit(solution)/shard_map/scatter-add | solution.py:38
  192.4 45.3 %scatter_fusion = f32[2,12289]{0,1:T(8,128)} fusion(f32[2,12289]{0,1:T(8,128)} %scatter_custom_fusion, s32[8192]{0:T(1024)S(1)} %get-tuple-element.30, f32[8192,2]{1,0:T(8,128)} %copy.91), kind=kCustom, calls=%fused_computation.5 | custom fusion | flops 16384 | bytes 229376 | tf_op jit(solution)/shard_map/scatter-add | solution.py:39
  240.7 3.3 all-to-all-start.1
  244.7 12.1 %psum.44 = f32[2,1024]{1,0:T(2,128)S(1)} all-reduce(f32[2,1024]{1,0:T(2,128)S(1)} %fusion), channel_id=1, replica_groups=mesh['anim'=8,'mark'=4] {'mark'}, use_global_device_ids=true, to_apply=%region_6.7 | all-reduce | flops 2048 | bytes 16384 | tf_op jit(solution)/shard_map/psum | solution.py:58
  257.0 4.5 %slice.106 = f32[2,8192]{0,1:T(8,128)} slice(f32[2,12289]{0,1:T(8,128)} %scatter_fusion), slice={[0:2], [0:8192]} | slice | bytes 131072 | tf_op jit(solution)/shard_map/slice | solution.py:44
  265.0 28.2 %scatter_custom_fusion.2 = f32[2,8193]{0,1:T(8,128)} fusion(s32[4096]{0:T(1024)S(1)} %bitcast.43, f32[4096,2]{1,0:T(8,128)S(1)} %copy.95, f32[]{:T(128)} %constant.12.clone.1), kind=kCustom, calls=%fused_computation.15 | custom fusion | flops 8192 | bytes 65548 | tf_op jit(solution)/shard_map/scatter-add | solution.py:43
  293.2 4.4 %slice.108 = f32[2,8192]{0,1:T(8,128)} slice(f32[2,8193]{0,1:T(8,128)} %scatter_custom_fusion.2), slice={[0:2], [0:8192]} | slice | bytes 131072 | tf_op jit(solution)/shard_map/slice | solution.py:44
  303.2 9.6 %scatter_fusion.1 = f32[2,8192]{0,1:T(8,128)} fusion(f32[2,8192]{0,1:T(8,128)} %copy.98, s32[1024]{0:T(1024)S(1)} %get-tuple-element.37, f32[1024,2]{1,0:T(8,128)S(1)} %copy.99), kind=kCustom, calls=%fused_computation.7 | custom fusion | flops 2048 | bytes 28672 | tf_op jit(solution)/shard_map/scatter-add | solution.py:59
  312.8 7.8 %fusion.17 = (f32[1,8192]{0,1:T(8,128)}, f32[1,8192]{0,1:T(8,128)}) fusion(f32[2,8192]{0,1:T(8,128)} %scatter_fusion.1), kind=kLoop, calls=%fused_computation.63 | loop fusion | bytes 131072 | tf_op jit(solution)/shard_map/slice | solution.py:14
  320.6 2.9 copy.104
  323.5 2.8 copy.105
  330.3 12.8 %all-reduce = (f32[]{:T(128)}, f32[]{:T(128)}, f32[]{:T(128)}, f32[]{:T(128)}) all-reduce(f32[]{:T(128)} %get-tuple-element.8, f32[]{:T(128)} %get-tuple-element.9, f32[]{:T(128)} %get-tuple-element.7, f32[]{:T(128)} %get-tuple-element.6), channel_id=1, replica_groups=mesh['anim'=8,'mark'=4] {'anim'}, use_global_device_ids=true, to_apply=%region_1.2 | all-reduce | flops 4 | bytes 32 | tf_op jit(solution)/shard_map/psum | solution.py:84
  (55 shorter events, 23.6 us)
Async XLA Ops:
  0.6 24.4 %copy-start = (f32[2,8192]{1,0:T(2,128)S(1)}, f32[2,8192]{1,0:T(2,128)}, u32[]{:S(2)}) copy-start(f32[2,8192]{1,0:T(2,128)} %param.15) | copy-start | bytes 196612
  0.6 24.3 %copy-start.8 = (f32[2048]{0:T(1024)S(1)}, f32[2048]{0:T(1024)}, u32[]{:S(2)}) copy-start(f32[2048]{0:T(1024)} %param.24) | copy-start | bytes 24580
  0.7 24.3 %copy-start.9 = (s32[1024]{0:T(1024)S(1)}, s32[1024]{0:T(1024)}, u32[]{:S(2)}) copy-start(s32[1024]{0:T(1024)} %param.22) | copy-start | bytes 12292
  0.7 24.3 %copy-start.2 = (s32[8192]{0:T(1024)S(1)}, s32[8192]{0:T(1024)}, u32[]{:S(2)}) copy-start(s32[8192]{0:T(1024)} %param.19) | copy-start | bytes 98308
  0.7 24.4 %copy-start.3 = (s32[8192]{0:T(1024)S(1)}, s32[8192]{0:T(1024)}, u32[]{:S(2)}) copy-start(s32[8192]{0:T(1024)} %param.20) | copy-start | bytes 98308
  0.7 24.4 %copy-start.4 = (f32[3,8192]{1,0:T(4,128)S(1)}, f32[3,8192]{1,0:T(4,128)}, u32[]{:S(2)}) copy-start(f32[3,8192]{1,0:T(4,128)} %param.16) | copy-start | bytes 294916
  19.8 51.2 %all-to-all-start = ((f32[2,8,512]{2,0,1:T(2,128)}), f32[2,8,512]{2,0,1:T(2,128)S(1)}, u32[]{:S(2)}, u32[]{:S(2)}) async-start(f32[2,8,512]{2,0,1:T(2,128)} %select_bitcast_fusion), calls=%async_computation | async-start | bytes 65536 | tf_op jit(solution)/shard_map/all_to_all | solution.py:25
  30.2 31.7 %copy-start.7 = (f32[2048]{0:T(1024)S(1)}, f32[2048]{0:T(1024)}, u32[]{:S(2)}) copy-start(f32[2048]{0:T(1024)} %param.25) | copy-start | bytes 24580
  192.4 51.6 %copy-start.10 = (f32[2,2]{1,0:T(2,128)S(1)}, f32[2,2]{1,0:T(2,128)}, u32[]{:S(2)}) copy-start(f32[2,2]{1,0:T(2,128)} %param.18) | copy-start | bytes 52
  240.7 23.7 %all-to-all-start.1 = ((f32[2,8,512]{2,0,1:T(2,128)}), f32[2,8,512]{2,0,1:T(2,128)S(1)}, u32[]{:S(2)}, u32[]{:S(2)}) async-start(f32[2,8,512]{2,0,1:T(2,128)} %copy.94), calls=%async_computation.1 | async-start | bytes 65536 | tf_op jit(solution)/shard_map/all_to_all | solution.py:41
  320.6 8.5 %copy-start.1 = (f32[2,8192]{1,0:T(2,128)S(1)}, f32[2,8192]{1,0:T(2,128)}, u32[]{:S(2)}) copy-start(f32[2,8192]{1,0:T(2,128)} %param.14) | copy-start | bytes 196612
  320.6 8.5 %copy-start.5 = (f32[3,8192]{1,0:T(4,128)S(1)}, f32[3,8192]{1,0:T(4,128)}, u32[]{:S(2)}) copy-start(f32[3,8192]{1,0:T(4,128)} %param.17) | copy-start | bytes 294916
  320.6 26.4 %copy-start.6 = (f32[2,8192]{1,0:T(2,128)S(1)}, f32[2,8192]{1,0:T(2,128)}, u32[]{:S(2)}) copy-start(f32[2,8192]{1,0:T(2,128)} %param.13) | copy-start | bytes 196612
where the time goes:
time: 349 us; the launch traced here: 348 us
  other arithmetic  138 us (40%)
  local copies, waits for them, and re-layouts  131 us (38%)
  blocking collectives  49.8 us (14%)
  matrix products  15.9 us (5%)
  starting transfers between devices  8.51 us (2%)
  between operations  4.82 us (1%)
    scatter-add x1, other arithmetic, pedigree_apply(): spread = spread.at[:, sire_index].add(-0.5 * sampling)  47.3 us
    scatter-add x1, other arithmetic, pedigree_apply(): spread = spread.at[:, dam_index].add(-0.5 * sampling)  45.3 us
    gather x2, local copies, waits for them, and re-layouts, pedigree_apply(): lookup_table[:, sire_index] + lookup_table[:, dam_index]  33.5 us
    gather x2, local copies, waits for them, and re-layouts, pedigree_apply(): lookup_table[:, dam_index]  33.5 us
    scatter-add x1, other arithmetic, pedigree_apply(): jnp.zeros((2, animals + 1), jnp.float32).at[:, target].add(inbound)  28.2 us
    psum x1, blocking collectives, genomic_apply(): marker_total = lax.psum(partial_markers, 'anim')  24.8 us
    unnamed x29, local copies, waits for them, and re-layouts  14.8 us
    gather x2, local copies, waits for them, and re-layouts, pedigree_apply(): direction[:, jnp.maximum(owned_rows, 0)]  13.6 us
  transfers between devices with their start and end apart: 2, of which 0 were waited for; matrix products, arithmetic and copies ran while one was open for 8% of the time, Pallas kernels for 0%

commit v1 on v0

v1 whole, which is shorter than its diff:
```python
import functools

import jax
import jax.numpy as jnp
from jax import lax
from jax.experimental import pallas as pl
from jax.experimental.pallas import tpu as pltpu
from jax.sharding import PartitionSpec as P

LANES = 128
WIDE = 256
STEP = 512
MESH = pl.DeviceIdType.MESH


def take(row, lane, like):
    table = jnp.broadcast_to(row, like.shape)
    return jnp.take_along_axis(table, lane, axis=1, mode="promise_in_bounds")


def split2(value):
    upper = value.astype(jnp.bfloat16).astype(jnp.float32)
    return upper, value - upper


def split3(value):
    upper, rest = split2(value)
    middle, lower = split2(rest)
    return upper, middle, lower


def scatter_product(index, values, height):
    high = index >> 8
    low = index & (WIDE - 1)
    count = index.shape[1]
    rows = lax.broadcasted_iota(jnp.int32, (height, count), 0) == high
    lanes = lax.broadcasted_iota(jnp.int32, (WIDE, count), 0) == low
    parts = []
    for value in values:
        for part in split2(value):
            parts.append(jnp.where(rows, part, 0.0).astype(jnp.bfloat16))
    left = jnp.concatenate(parts, axis=0)
    right = jnp.where(lanes, 1.0, 0.0).astype(jnp.bfloat16)
    return lax.dot_general(
        left, right, (((1,), (1,)), ((), ())), preferred_element_type=jnp.float32
    )


def kernel(
    blocks,
    layers,
    direction,
    residual,
    record_inverse,
    precondition,
    genetic,
    sire,
    dam,
    sire_flat,
    dam_flat,
    send_rows,
    picked_row,
    picked_flat,
    freq,
    weight,
    genotypes,
    image_out,
    coef_out,
    codes,
    codes_half,
    table,
    outgoing,
    ghosts,
    outbound,
    inbound,
    sampling,
    spread,
    gathered,
    marker_parts,
    row_parts,
    dots,
    code_sem,
    ghost_send,
    ghost_recv,
    back_send,
    back_recv,
    marker_send,
    marker_recv,
    row_send,
    row_recv,
    dot_send,
    dot_recv,
):
    animals = direction.shape[1]
    rows = animals // LANES
    capacity = send_rows.shape[1]
    spots = capacity // LANES
    gen_rows = picked_row.shape[0]
    markers = freq.shape[1]
    local_high = animals // WIDE
    full_high = local_high + blocks * capacity // WIDE
    chunks = codes.shape[0]
    chunk_rows = codes.shape[1]
    me = lax.axis_index("anim")
    layer = lax.axis_index("mark")

    def fetch(c):
        return pltpu.make_async_copy(
            genotypes.at[pl.ds(c * chunk_rows, chunk_rows)], codes.at[c], code_sem.at[c]
        )

    for c in range(chunks):
        fetch(c).start()

    barrier = pltpu.get_barrier_semaphore()
    for off in range(1, blocks):
        pl.semaphore_signal(
            barrier, inc=1, device_id={"anim": lax.rem(me + off, blocks)}, device_id_type=MESH
        )
    for off in range(1, layers):
        pl.semaphore_signal(
            barrier, inc=1, device_id={"mark": lax.rem(layer + off, layers)}, device_id_type=MESH
        )

    def spread_out(axis, size, mine, buffer_from, buffer_to, send_sem, recv_sem, by_target):
        copies = []
        for off in range(1, size):
            peer = lax.rem(mine + off, size)
            copy = pltpu.make_async_remote_copy(
                src_ref=buffer_from.at[peer] if by_target else buffer_from.at[mine],
                dst_ref=buffer_to.at[mine],
                send_sem=send_sem.at[off - 1],
                recv_sem=recv_sem.at[mine],
                device_id={axis: peer},
                device_id_type=MESH,
            )
            copy.start()
            copies.append(copy)
        return copies

    def arrive(axis, size, mine, buffer, send_sem, recv_sem):
        for off in range(1, size):
            peer = lax.rem(mine + off, size)
            pltpu.make_async_remote_copy(
                src_ref=buffer.at[peer],
                dst_ref=buffer.at[peer],
                send_sem=send_sem.at[off - 1],
                recv_sem=recv_sem.at[peer],
                device_id={axis: peer},
                device_id_type=MESH,
            ).wait_recv()

    for r in range(rows):
        pair = direction[:, r * LANES : (r + 1) * LANES]
        table[0, r : r + 1, :] = pair[0:1]
        table[1, r : r + 1, :] = pair[1:2]

    wanted = [send_rows[:, k * LANES : (k + 1) * LANES] for k in range(spots)]
    wanted.append(picked_row[...])
    wanted_high = [index >> 7 for index in wanted]
    wanted_lane = [index & (LANES - 1) for index in wanted]

    def pick_wanted(r, found):
        out = []
        for high, lane, (first, second) in zip(wanted_high, wanted_lane, found):
            here = high == r
            out.append(
                (
                    jnp.where(here, take(table[0, pl.ds(r, 1), :], lane, lane), first),
                    jnp.where(here, take(table[1, pl.ds(r, 1), :], lane, lane), second),
                )
            )
        return tuple(out)

    zeros = tuple((jnp.zeros(i.shape, jnp.float32),) * 2 for i in wanted)
    found = lax.fori_loop(0, rows, pick_wanted, zeros, unroll=4)
    for k in range(spots):
        for trait in range(2):
            for b in range(blocks):
                outgoing[b, trait * spots + k : trait * spots + k + 1, :] = found[k][trait][b : b + 1]
    picked = found[spots]

    pl.semaphore_wait(barrier, blocks - 1 + layers - 1)
    ghost_copies = spread_out("anim", blocks, me, outgoing, ghosts, ghost_send, ghost_recv, True)
    ghosts[me] = jnp.zeros(ghosts.shape[1:], jnp.float32)

    picked_parts = [split3(value) for value in picked]
    total = jnp.zeros((6, markers), jnp.float32)
    per_chunk = chunk_rows // LANES
    for c in range(chunks):
        fetch(c).wait()
        codes_half[pl.ds(c * chunk_rows, chunk_rows), :] = (
            codes[c].astype(jnp.float32).astype(jnp.bfloat16)
        )
        lines = []
        for part in range(3):
            for trait in range(2):
                block = picked_parts[trait][part]
                lines.append(
                    jnp.concatenate(
                        [block[c * per_chunk + i : c * per_chunk + i + 1] for i in range(per_chunk)],
                        axis=1,
                    )
                )
        left = jnp.concatenate(lines, axis=0).astype(jnp.bfloat16)
        total = total + jnp.dot(
            left,
            codes_half[pl.ds(c * chunk_rows, chunk_rows), :],
            preferred_element_type=jnp.float32,
        )
    frequency = 2.0 * freq[...]
    sums = [jnp.sum(picked[trait]) for trait in range(2)]
    marker_parts[me] = jnp.concatenate(
        [
            (total[t : t + 1] + total[2 + t : 3 + t] + total[4 + t : 5 + t]) - sums[t] * frequency
            for t in range(2)
        ],
        axis=0,
    )
    marker_copies = spread_out(
        "anim", blocks, me, marker_parts, marker_parts, marker_send, marker_recv, False
    )

    slots = [sire[...], dam[...]]
    sums_of_parents = [jnp.zeros((rows, LANES), jnp.float32)] * 2
    known = (slots[0] >= 0).astype(jnp.float32) + (slots[1] >= 0).astype(jnp.float32)
    parents = []
    for slot in slots:
        high = slot >> 7
        lane = slot & (LANES - 1)

        def local(r, carry, high=high, lane=lane):
            here = high == r
            return tuple(
                jnp.where(here, take(table[t, pl.ds(r, 1), :], lane, lane), carry[t])
                for t in range(2)
            )

        zero = jnp.zeros((rows, LANES), jnp.float32)
        parents.append(lax.fori_loop(0, rows, local, (zero, zero), unroll=2))
    arrive("anim", blocks, me, ghosts, ghost_send, ghost_recv)
    for which, slot in enumerate(slots):
        high = slot >> 7
        lane = slot & (LANES - 1)

        def remote(source, carry, high=high, lane=lane):
            for k in range(spots):
                here = high == rows + source * spots + k
                carry = tuple(
                    jnp.where(
                        here,
                        take(ghosts[source, t * spots + k : t * spots + k + 1, :], lane, lane),
                        carry[t],
                    )
                    for t in range(2)
                )
            return carry

        parents[which] = lax.fori_loop(0, blocks, remote, parents[which])
    factor = 1.0 / (1.0 - 0.25 * known)
    for t in range(2):
        sampling[t] = factor * (table[t] - 0.5 * (parents[0][t] + parents[1][t]))

    spread[...] = jnp.zeros(spread.shape, jnp.float32)
    lines_per_step = STEP // LANES

    def sampling_lines(t, j):
        return jnp.concatenate(
            [sampling[t, pl.ds(j * lines_per_step + i, 1), :] for i in range(lines_per_step)], axis=1
        )

    def offspring(j, carry):
        values = [-0.5 * sampling_lines(t, j) for t in range(2)]
        at = pl.ds(pl.multiple_of(j * STEP, STEP), STEP)
        spread[...] += scatter_product(sire_flat[:, at], values, full_high) + scatter_product(
            dam_flat[:, at], values, full_high
        )
        return carry

    lax.fori_loop(0, animals // STEP, offspring, 0)
    per_source = capacity // WIDE
    for t in range(2):
        both = spread[2 * t * full_high : (2 * t + 1) * full_high] + spread[
            (2 * t + 1) * full_high : (2 * t + 2) * full_high
        ]
        gathered[t] = both[:local_high]
        for b in range(blocks):
            for i in range(per_source):
                h = local_high + b * per_source + i
                for half in range(2):
                    at = t * spots + 2 * i + half
                    outbound[b, at : at + 1, :] = both[h : h + 1, half * LANES : (half + 1) * LANES]
    back_copies = spread_out("anim", blocks, me, outbound, inbound, back_send, back_recv, True)
    inbound[me] = jnp.zeros(inbound.shape[1:], jnp.float32)

    arrive("anim", blocks, me, marker_parts, marker_send, marker_recv)
    marker_total = marker_parts[0]
    for b in range(1, blocks):
        marker_total = marker_total + marker_parts[b]
    scaled = marker_total * weight[...] / (markers * layers)
    offset = jnp.sum(scaled * frequency, axis=1, keepdims=True)
    left = jnp.concatenate(split3(scaled), axis=0).astype(jnp.bfloat16)
    row_sums = lax.dot_general(
        left, codes_half[...], (((1,), (1,)), ((), ())), preferred_element_type=jnp.float32
    )
    row_parts[layer] = row_sums[0:2] + row_sums[2:4] + row_sums[4:6] - offset
    row_copies = spread_out("mark", layers, layer, row_parts, row_parts, row_send, row_recv, False)

    arrive("anim", blocks, me, inbound, back_send, back_recv)

    def returned(b, carry):
        values = [
            jnp.concatenate(
                [inbound[b, t * spots + k : t * spots + k + 1, :] for k in range(spots)], axis=1
            )
            for t in range(2)
        ]
        return carry + scatter_product(send_rows[pl.ds(b, 1), :], values, local_high)

    added = lax.fori_loop(0, blocks, returned, jnp.zeros((4 * local_high, WIDE), jnp.float32))
    arrive("mark", layers, layer, row_parts, row_send, row_recv)
    genomic = row_parts[0]
    for z in range(1, layers):
        genomic = genomic + row_parts[z]
    added = added + scatter_product(picked_flat[...], [genomic[0:1], genomic[1:2]], local_high)
    for t in range(2):
        gathered[t] = (
            gathered[t]
            + added[2 * t * local_high : (2 * t + 1) * local_high]
            + added[(2 * t + 1) * local_high : (2 * t + 2) * local_high]
        )

    g00, g01, g10, g11 = genetic[0, 0], genetic[0, 1], genetic[1, 0], genetic[1, 1]

    def finish(j, carry):
        at = pl.ds(pl.multiple_of(j * STEP, STEP), STEP)
        d = direction[:, at]
        r = residual[:, at]
        rec = record_inverse[:, at]
        pre = precondition[:, at]
        d0, d1, r0, r1 = d[0:1], d[1:2], r[0:1], r[1:2]
        terms = [
            sampling_lines(t, j)
            + jnp.concatenate(
                [gathered[t, pl.ds(j * (STEP // WIDE) + i, 1), :] for i in range(STEP // WIDE)],
                axis=1,
            )
            for t in range(2)
        ]
        i0 = rec[0:1] * d0 + rec[1:2] * d1 + (g00 * terms[0] + g01 * terms[1])
        i1 = rec[1:2] * d0 + rec[2:3] * d1 + (g10 * terms[0] + g11 * terms[1])
        image_out[0:1, at] = i0
        image_out[1:2, at] = i1
        s0 = pre[0:1] * r0 + pre[1:2] * r1
        s1 = pre[1:2] * r0 + pre[2:3] * r1
        m0 = pre[0:1] * i0 + pre[1:2] * i1
        m1 = pre[1:2] * i0 + pre[2:3] * i1
        old, curve, cross, image = carry
        return (
            old + (r0 * s0 + r1 * s1),
            curve + (d0 * i0 + d1 * i1),
            cross + (i0 * s0 + i1 * s1),
            image + (i0 * m0 + i1 * m1),
        )

    zero = jnp.zeros((1, STEP), jnp.float32)
    products = lax.fori_loop(0, animals // STEP, finish, (zero,) * 4)
    lines = [
        sum(value[:, i * LANES : (i + 1) * LANES] for i in range(STEP // LANES))
        for value in products
    ]
    lines.append(jnp.zeros((4, LANES), jnp.float32))
    dots[me] = jnp.concatenate(lines, axis=0)
    dot_copies = spread_out("anim", blocks, me, dots, dots, dot_send, dot_recv, False)
    arrive("anim", blocks, me, dots, dot_send, dot_recv)
    whole = dots[0]
    for b in range(1, blocks):
        whole = whole + dots[b]
    sums = jnp.sum(whole, axis=1, keepdims=True)
    old, curve, cross, image = (sums[i : i + 1] for i in range(4))
    step = old / curve
    new = old - 2.0 * step * cross + step * step * image
    coef_out[...] = jnp.broadcast_to(jnp.concatenate([step, new / old], axis=0), coef_out.shape)
    for copy in ghost_copies + marker_copies + back_copies + row_copies + dot_copies:
        copy.wait_send()


def on_device(
    blocks,
    layers,
    solution,
    residual,
    direction,
    record_inverse,
    precondition,
    genetic_inverse,
    sire_slot,
    dam_slot,
    send_rows,
    genotyped_row,
    genotypes,
    allele_freq,
    marker_weight,
):
    animals = direction.shape[1]
    rows = animals // LANES
    capacity = send_rows.shape[2]
    gen, markers = genotypes.shape
    chunk_rows = 256
    lists = (blocks, 2 * capacity // LANES, LANES)
    full_high = (animals + blocks * capacity) // WIDE
    vmem = pl.BlockSpec(memory_space=pltpu.VMEM)
    dma = pltpu.SemaphoreType.DMA
    f32 = jnp.float32
    image, coef = pl.pallas_call(
        functools.partial(kernel, blocks, layers),
        out_shape=(
            jax.ShapeDtypeStruct((2, animals), f32),
            jax.ShapeDtypeStruct((2, LANES), f32),
        ),
        in_specs=[vmem] * 4
        + [pl.BlockSpec(memory_space=pltpu.SMEM)]
        + [vmem] * 9
        + [pl.BlockSpec(memory_space=pl.ANY)],
        out_specs=(vmem, vmem),
        scratch_shapes=[
            pltpu.VMEM((gen // chunk_rows, chunk_rows, markers), jnp.int32),
            pltpu.VMEM((gen, markers), jnp.bfloat16),
            pltpu.VMEM((2, rows, LANES), f32),
            pltpu.VMEM(lists, f32),
            pltpu.VMEM(lists, f32),
            pltpu.VMEM(lists, f32),
            pltpu.VMEM(lists, f32),
            pltpu.VMEM((2, rows, LANES), f32),
            pltpu.VMEM((4 * full_high, WIDE), f32),
            pltpu.VMEM((2, animals // WIDE, WIDE), f32),
            pltpu.VMEM((blocks, 2, markers), f32),
            pltpu.VMEM((layers, 2, gen), f32),
            pltpu.VMEM((blocks, 8, LANES), f32),
            dma((gen // chunk_rows,)),
            dma((blocks - 1,)),
            dma((blocks,)),
            dma((blocks - 1,)),
            dma((blocks,)),
            dma((blocks - 1,)),
            dma((blocks,)),
            dma((layers - 1,)),
            dma((layers,)),
            dma((blocks - 1,)),
            dma((blocks,)),
        ],
        compiler_params=pltpu.CompilerParams(
            collective_id=0, has_side_effects=True, vmem_limit_bytes=50 * 2**20
        ),
    )(
        direction,
        residual,
        record_inverse,
        precondition,
        genetic_inverse,
        sire_slot.reshape(rows, LANES),
        dam_slot.reshape(rows, LANES),
        sire_slot.reshape(1, animals),
        dam_slot.reshape(1, animals),
        send_rows.reshape(blocks, capacity),
        genotyped_row.reshape(gen // LANES, LANES),
        genotyped_row.reshape(1, gen),
        allele_freq.reshape(1, markers),
        marker_weight.reshape(1, markers),
        genotypes,
    )
    step = coef[0, 0]
    ratio = coef[1, 0]
    new_residual = residual - step * image
    upper = precondition[0] * new_residual[0] + precondition[1] * new_residual[1]
    lower = precondition[1] * new_residual[0] + precondition[2] * new_residual[1]
    return (
        solution + step * direction,
        new_residual,
        jnp.stack([upper, lower]) + ratio * direction,
    )


def solution(mesh):
    return jax.shard_map(
        functools.partial(on_device, mesh.shape["anim"], mesh.shape["mark"]),
        mesh=mesh,
        in_specs=(
            P(None, "anim"),
            P(None, "anim"),
            P(None, "anim"),
            P(None, "anim"),
            P(None, "anim"),
            P(),
            P("anim"),
            P("anim"),
            P("anim", None, None),
            P("anim"),
            P("anim", "mark"),
            P("mark"),
            P("mark"),
        ),
        out_specs=(P(None, "anim"), P(None, "anim"), P(None, "anim")),
        check_vma=False,
    )
```

time: 349 us -> 50.8 us (0.15)
  other arithmetic: 138 us -> 2.61 us
  local copies, waits for them, and re-layouts: 131 us -> 9.02 us
  blocking collectives: 49.8 us -> 0 us
  Pallas kernels: 0 us -> 37.8 us
  matrix products: 15.9 us -> 0 us
  starting transfers between devices: 8.51 us -> 0 us
  between operations: 4.82 us -> 0.7 us
    scatter-add x4 -> x0, other arithmetic: 130 us -> none  [the longest x1 47.3 us: pedigree_apply(): spread = spread.at[:, sire_index].add(-0.5 * sampling)]
    gather x7 -> x0, local copies, waits for them, and re-layouts: 85.6 us -> none  [the longest x2 33.5 us: pedigree_apply(): lookup_table[:, sire_index] + lookup_table[:, dam_index]]
    psum x3 -> x0, blocking collectives: 49.8 us -> none  [the longest x1 24.8 us: genomic_apply(): marker_total = lax.psum(partial_markers, 'anim')]
    pallas_call x0 -> x1, Pallas kernels: none -> 37.8 us  [on_device(): pl.pallas_call(functools.partial(kernel, blocks, layers), out_shape=(jax....]
    slice x5 -> x1, local copies, waits for them, and re-layouts: 19.1 us -> 0.54 us  [on_device(): ratio = coef[1, 0]]
    dot_general x2 -> x0, matrix products: 15.9 us -> none  [the longest x1 9.06 us: genomic_apply(): lax.dot_general(scaled, centered, (((1,), (1,)), ((), ())), precision=lax...]
    all_to_all x2 -> x0, starting transfers between devices: 8.51 us -> none  [the longest x1 5.17 us: pedigree_apply(): lax.all_to_all(outgoing, 'anim', split_axis=1, concat_axis=1, tiled=True)]
    unnamed x29 -> x26, local copies, waits for them, and re-layouts: 14.8 us -> 8.48 us
  transfers between devices with their start and end apart: 2 -> 0, of which waited for: 0 -> 0; matrix products, arithmetic and copies ran while one was open for 8% -> 0% of each run, Pallas kernels for 0% -> 0%
where the time goes in v1:
time: 50.8 us; the launch traced here: 50.2 us
  Pallas kernels  37.8 us (74%)
  local copies, waits for them, and re-layouts  9.02 us (18%)
  other arithmetic  2.61 us (5%)
  between operations  0.7 us (1%)
    pallas_call x1, Pallas kernels, on_device(): pl.pallas_call(functools.partial(kernel, blocks, layers), out_shape=(jax....  37.8 us
    unnamed x26, local copies, waits for them, and re-layouts  8.48 us
    add x1, other arithmetic, on_device(): jnp.stack([upper, lower]) + ratio * direction  1.93 us

profile of v1, /device:TPU:0, one launch (start us, length us, event | category | flops | bytes accessed | tf_op | source)
XLA Modules:
  0.0 50.2 jit_solution(9829456300978596038)
XLA Ops:
  0.6 0.0 copy-start
  0.6 0.9 %copy-done = f32[3,8192]{1,0:T(4,128)S(1)} copy-done((f32[3,8192]{1,0:T(4,128)S(1)}, f32[3,8192]{1,0:T(4,128)}, u32[]{:S(2)}) %copy-start) | copy-done | bytes 98328
  1.5 0.0 copy-start.1
  1.5 0.8 %copy-done.1 = f32[2,8192]{1,0:T(2,128)S(1)} copy-done((f32[2,8192]{1,0:T(2,128)S(1)}, f32[2,8192]{1,0:T(2,128)}, u32[]{:S(2)}) %copy-start.1) | copy-done | bytes 65560
  2.4 0.0 copy-start.2
  2.4 0.8 %copy-done.2 = f32[2,8192]{1,0:T(2,128)S(1)} copy-done((f32[2,8192]{1,0:T(2,128)S(1)}, f32[2,8192]{1,0:T(2,128)}, u32[]{:S(2)}) %copy-start.2) | copy-done | bytes 65560
  3.2 0.0 copy-start.3
  3.2 0.9 %copy-done.3 = f32[3,8192]{1,0:T(4,128)S(1)} copy-done((f32[3,8192]{1,0:T(4,128)S(1)}, f32[3,8192]{1,0:T(4,128)}, u32[]{:S(2)}) %copy-start.3) | copy-done | bytes 98328
  4.1 0.0 copy-start.4
  4.1 0.8 %copy-done.4 = s32[8192]{0:T(1024)S(1)} copy-done((s32[8192]{0:T(1024)S(1)}, s32[8192]{0:T(1024)}, u32[]{:S(2)}) %copy-start.4) | copy-done | bytes 32792
  4.9 0.8 %copy-done.5 = s32[8192]{0:T(1024)S(1)} copy-done((s32[8192]{0:T(1024)S(1)}, s32[8192]{0:T(1024)}, u32[]{:S(2)}) %copy-start.5) | copy-done | bytes 32792
  5.6 0.7 %copy-done.6 = s32[1,8,512]{2,1,0:T(8,128)S(1)} copy-done((s32[1,8,512]{2,1,0:T(8,128)S(1)}, s32[1,8,512]{2,1,0:T(8,128)}, u32[]{:S(2)}) %copy-start.6) | copy-done | bytes 16408
  6.4 0.7 %copy-done.7 = s32[1024]{0:T(1024)S(1)} copy-done((s32[1024]{0:T(1024)S(1)}, s32[1024]{0:T(1024)}, u32[]{:S(2)}) %copy-start.7) | copy-done | bytes 4120
  7.0 0.7 %copy-done.8 = f32[2048]{0:T(1024)S(1)} copy-done((f32[2048]{0:T(1024)S(1)}, f32[2048]{0:T(1024)}, u32[]{:S(2)}) %copy-start.8) | copy-done | bytes 8216
  7.7 0.7 %copy-done.9 = f32[2048]{0:T(1024)S(1)} copy-done((f32[2048]{0:T(1024)S(1)}, f32[2048]{0:T(1024)}, u32[]{:S(2)}) %copy-start.9) | copy-done | bytes 8216
  8.4 0.7 %copy-done.10 = f32[2,2]{1,0:T(2,128)S(1)} copy-done((f32[2,2]{1,0:T(2,128)S(1)}, f32[2,2]{1,0:T(2,128)}, u32[]{:S(2)}) %copy-start.10) | copy-done | bytes 40
  9.1 37.8 %shard_map.148 = (f32[2,8192]{1,0:T(2,128)S(1)}, f32[2,128]{1,0:T(2,128)S(1)}) custom-call(f32[2,8192]{1,0:T(2,128)S(1)} %copy-done.2, f32[2,8192]{1,0:T(2,128)S(1)} %copy-done.1, f32[3,8192]{1,0:T(4,128)S(1)} %copy-done.3, f32[3,8192]{1,0:T(4,128)S(1)} %copy-done, f32[2,2]{1,0:T(2,128)S(1)} %copy-done.10, s32[64,128]{1,0:T(8,128)S(1)} %bitcast.11, ...), custom_call_target="tpu_custom_call" | custom-call | tf_op jit(solution)/shard_map/pallas_call | solution.py:415
  47.0 0.5 %fusion = (f32[1,1]{1,0:T(1,128)}, f32[1,1]{1,0:T(1,128)}) fusion(f32[2,128]{1,0:T(2,128)S(1)} %get-tuple-element.5), kind=kLoop, calls=%fused_computation.5 | loop fusion | bytes 16 | tf_op jit(solution)/shard_map/slice | solution.py:473
  47.5 0.6 %multiply_subtract_fusion = f32[2,8192]{1,0:T(2,128)S(1)} fusion(f32[2,8192]{1,0:T(2,128)S(1)} %copy-done.1, f32[2,8192]{1,0:T(2,128)S(1)} %get-tuple-element.6, f32[]{:T(128)} %bitcast.9), kind=kLoop, calls=%fused_computation.1 | loop fusion | flops 32768 | bytes 196612 | tf_op jit(solution)/shard_map/sub | solution.py:474
  48.1 0.0 copy-start.11
  48.1 0.1 multiply_add_fusion.2
  48.2 0.0 copy-done.12
  48.2 1.9 %maximum_add_fusion = (f32[2,8192]{1,0:T(2,128)}, f32[2,8192]{1,0:T(2,128)}) fusion(f32[1,8192]{1,0:T(1,128)S(1)} %get-tuple-element.8, f32[1,8192]{1,0:T(1,128)S(1)} %get-tuple-element.7, f32[2,8192]{1,0:T(2,128)S(1)} %copy-done.2, f32[]{:T(128)} %bitcast.10, f32[2,8192]{1,0:T(2,128)S(1)} %copy-done.12, f32[]{:T(128)} %bitcast.9), kind=kLoop, calls=%fused_computation | loop fusion | flops 81920 | bytes 327688 | tf_op jit(solution)/shard_map/add | solution.py:480
  50.2 0.0 copy-done.11
  (7 shorter events, 0.0 us)
Async XLA Ops:
  0.6 0.9 %copy-start = (f32[3,8192]{1,0:T(4,128)S(1)}, f32[3,8192]{1,0:T(4,128)}, u32[]{:S(2)}) copy-start(f32[3,8192]{1,0:T(4,128)} %precondition.1) | copy-start | bytes 294916
  1.5 0.8 %copy-start.1 = (f32[2,8192]{1,0:T(2,128)S(1)}, f32[2,8192]{1,0:T(2,128)}, u32[]{:S(2)}) copy-start(f32[2,8192]{1,0:T(2,128)} %residual.1) | copy-start | bytes 196612
  2.4 0.8 %copy-start.2 = (f32[2,8192]{1,0:T(2,128)S(1)}, f32[2,8192]{1,0:T(2,128)}, u32[]{:S(2)}) copy-start(f32[2,8192]{1,0:T(2,128)} %direction.1) | copy-start | bytes 196612
  3.2 0.9 %copy-start.3 = (f32[3,8192]{1,0:T(4,128)S(1)}, f32[3,8192]{1,0:T(4,128)}, u32[]{:S(2)}) copy-start(f32[3,8192]{1,0:T(4,128)} %record_inverse.1) | copy-start | bytes 294916
  4.1 0.8 %copy-start.4 = (s32[8192]{0:T(1024)S(1)}, s32[8192]{0:T(1024)}, u32[]{:S(2)}) copy-start(s32[8192]{0:T(1024)} %param.19) | copy-start | bytes 98308
  4.9 0.8 %copy-start.5 = (s32[8192]{0:T(1024)S(1)}, s32[8192]{0:T(1024)}, u32[]{:S(2)}) copy-start(s32[8192]{0:T(1024)} %param.20) | copy-start | bytes 98308
  5.6 0.7 %copy-start.6 = (s32[1,8,512]{2,1,0:T(8,128)S(1)}, s32[1,8,512]{2,1,0:T(8,128)}, u32[]{:S(2)}) copy-start(s32[1,8,512]{2,1,0:T(8,128)} %param.21) | copy-start | bytes 49156
  6.4 0.7 %copy-start.7 = (s32[1024]{0:T(1024)S(1)}, s32[1024]{0:T(1024)}, u32[]{:S(2)}) copy-start(s32[1024]{0:T(1024)} %param.22) | copy-start | bytes 12292
  7.0 0.7 %copy-start.8 = (f32[2048]{0:T(1024)S(1)}, f32[2048]{0:T(1024)}, u32[]{:S(2)}) copy-start(f32[2048]{0:T(1024)} %param.24) | copy-start | bytes 24580
  7.7 0.7 %copy-start.9 = (f32[2048]{0:T(1024)S(1)}, f32[2048]{0:T(1024)}, u32[]{:S(2)}) copy-start(f32[2048]{0:T(1024)} %param.25) | copy-start | bytes 24580
  8.4 0.7 %copy-start.10 = (f32[2,2]{1,0:T(2,128)S(1)}, f32[2,2]{1,0:T(2,128)}, u32[]{:S(2)}) copy-start(f32[2,2]{1,0:T(2,128)} %genetic.1) | copy-start | bytes 52
  9.1 39.1 %copy-start.12 = (f32[2,8192]{1,0:T(2,128)S(1)}, f32[2,8192]{1,0:T(2,128)}, u32[]{:S(2)}) copy-start(f32[2,8192]{1,0:T(2,128)} %param.13) | copy-start | bytes 196612
  48.1 2.1 %copy-start.11 = (f32[2,8192]{1,0:T(2,128)}, f32[2,8192]{1,0:T(2,128)S(1)}, u32[]{:S(2)}) copy-start(f32[2,8192]{1,0:T(2,128)S(1)} %multiply_subtract_fusion) | copy-start | bytes 196612

commit v2 on v1

--- a/solution.py
+++ b/solution.py
@@ -49,10 +49,29 @@
 def kernel(
     blocks,
     layers,
+    direction_hbm,
+    residual_hbm,
+    record_inverse_hbm,
+    precondition_hbm,
+    genetic_hbm,
+    sire_hbm,
+    dam_hbm,
+    sire_flat_hbm,
+    dam_flat_hbm,
+    send_rows_hbm,
+    picked_row_hbm,
+    picked_flat_hbm,
+    freq_hbm,
+    weight_hbm,
+    genotypes,
+    solution_hbm,
+    image_out,
+    coef_out,
     direction,
     residual,
+    precondition,
+    solution,
     record_inverse,
-    precondition,
     genetic,
     sire,
     dam,
@@ -63,9 +82,7 @@
     picked_flat,
     freq,
     weight,
-    genotypes,
-    image_out,
-    coef_out,
+    input_sem,
     codes,
     codes_half,
     table,
@@ -109,8 +126,34 @@
             genotypes.at[pl.ds(c * chunk_rows, chunk_rows)], codes.at[c], code_sem.at[c]
         )
 
+    loads = [
+        pltpu.make_async_copy(source, target, input_sem.at[i])
+        for i, (source, target) in enumerate(
+            [
+                (direction_hbm, direction),
+                (send_rows_hbm, send_rows),
+                (picked_row_hbm, picked_row),
+                (freq_hbm, freq),
+                (sire_hbm, sire),
+                (dam_hbm, dam),
+                (sire_flat_hbm, sire_flat),
+                (dam_flat_hbm, dam_flat),
+                (weight_hbm, weight),
+                (picked_flat_hbm, picked_flat),
+                (genetic_hbm, genetic),
+                (record_inverse_hbm, record_inverse),
+                (residual_hbm, residual),
+                (precondition_hbm, precondition),
+                (solution_hbm, solution),
+            ]
+        )
+    ]
+    for load in loads[:4]:
+        load.start()
     for c in range(chunks):
         fetch(c).start()
+    for load in loads[4:]:
+        load.start()
 
     barrier = pltpu.get_barrier_semaphore()
     for off in range(1, blocks):
@@ -150,6 +193,8 @@
                 device_id_type=MESH,
             ).wait_recv()
 
+    for load in loads[:3]:
+        load.wait()
     for r in range(rows):
         pair = direction[:, r * LANES : (r + 1) * LANES]
         table[0, r : r + 1, :] = pair[0:1]
@@ -208,6 +253,7 @@
             codes_half[pl.ds(c * chunk_rows, chunk_rows), :],
             preferred_element_type=jnp.float32,
         )
+    loads[3].wait()
     frequency = 2.0 * freq[...]
     sums = [jnp.sum(picked[trait]) for trait in range(2)]
     marker_parts[me] = jnp.concatenate(
@@ -221,6 +267,8 @@
         "anim", blocks, me, marker_parts, marker_parts, marker_send, marker_recv, False
     )
 
+    for load in loads[4:8]:
+        load.wait()
     slots = [sire[...], dam[...]]
     sums_of_parents = [jnp.zeros((rows, LANES), jnp.float32)] * 2
     known = (slots[0] >= 0).astype(jnp.float32) + (slots[1] >= 0).astype(jnp.float32)
@@ -294,6 +342,7 @@
     inbound[me] = jnp.zeros(inbound.shape[1:], jnp.float32)
 
     arrive("anim", blocks, me, marker_parts, marker_send, marker_recv)
+    loads[8].wait()
     marker_total = marker_parts[0]
     for b in range(1, blocks):
         marker_total = marker_total + marker_parts[b]
@@ -318,6 +367,8 @@
         return carry + scatter_product(send_rows[pl.ds(b, 1), :], values, local_high)
 
     added = lax.fori_loop(0, blocks, returned, jnp.zeros((4 * local_high, WIDE), jnp.float32))
+    for load in loads[9:]:
+        load.wait()
     arrive("mark", layers, layer, row_parts, row_send, row_recv)
     genomic = row_parts[0]
     for z in range(1, layers):
@@ -330,7 +381,7 @@
             + added[(2 * t + 1) * local_high : (2 * t + 2) * local_high]
         )
 
-    g00, g01, g10, g11 = genetic[0, 0], genetic[0, 1], genetic[1, 0], genetic[1, 1]
+    g00, g01, g10, g11 = (genetic[a : a + 1, b : b + 1] for a in range(2) for b in range(2))
 
     def finish(j, carry):
         at = pl.ds(pl.multiple_of(j * STEP, STEP), STEP)
@@ -385,6 +436,23 @@
         copy.wait_send()
 
 
+def update(
+    image, coef, direction, residual, precondition, solution, new_solution, new_residual, new_direction
+):
+    step = coef[0:1, 0:1]
+    ratio = coef[1:2, 0:1]
+    for start in range(0, image.shape[1], STEP):
+        at = slice(start, start + STEP)
+        d = direction[:, at]
+        left = residual[:, at] - step * image[:, at]
+        pre = precondition[:, at]
+        new_solution[:, at] = solution[:, at] + step * d
+        new_residual[:, at] = left
+        scaled = ratio * d
+        new_direction[0:1, at] = pre[0:1] * left[0:1] + pre[1:2] * left[1:2] + scaled[0:1]
+        new_direction[1:2, at] = pre[1:2] * left[0:1] + pre[2:3] * left[1:2] + scaled[1:2]
+
+
 def on_device(
     blocks,
     layers,
@@ -412,18 +480,34 @@
     vmem = pl.BlockSpec(memory_space=pltpu.VMEM)
     dma = pltpu.SemaphoreType.DMA
     f32 = jnp.float32
-    image, coef = pl.pallas_call(
+    pair = pltpu.VMEM((2, animals), f32)
+    triple = pltpu.VMEM((3, animals), f32)
+    hbm = lambda value: pltpu.with_memory_space_constraint(value, pltpu.HBM)
+    carried = pl.pallas_call(
         functools.partial(kernel, blocks, layers),
         out_shape=(
-            jax.ShapeDtypeStruct((2, animals), f32),
-            jax.ShapeDtypeStruct((2, LANES), f32),
+            pair,
+            pltpu.VMEM((2, LANES), f32),
+            pair,
+            pair,
+            triple,
+            pair,
         ),
-        in_specs=[vmem] * 4
-        + [pl.BlockSpec(memory_space=pltpu.SMEM)]
-        + [vmem] * 9
-        + [pl.BlockSpec(memory_space=pl.ANY)],
-        out_specs=(vmem, vmem),
+        in_specs=[pl.BlockSpec(memory_space=pltpu.HBM)] * 16,
+        out_specs=(vmem,) * 6,
         scratch_shapes=[
+            pltpu.VMEM((3, animals), f32),
+            pltpu.VMEM((2, 2), f32),
+            pltpu.VMEM((rows, LANES), jnp.int32),
+            pltpu.VMEM((rows, LANES), jnp.int32),
+            pltpu.VMEM((1, animals), jnp.int32),
+            pltpu.VMEM((1, animals), jnp.int32),
+            pltpu.VMEM((blocks, capacity), jnp.int32),
+            pltpu.VMEM((gen // LANES, LANES), jnp.int32),
+            pltpu.VMEM((1, gen), jnp.int32),
+            pltpu.VMEM((1, markers), f32),
+            pltpu.VMEM((1, markers), f32),
+            dma((15,)),
             pltpu.VMEM((gen // chunk_rows, chunk_rows, markers), jnp.int32),
             pltpu.VMEM((gen, markers), jnp.bfloat16),
             pltpu.VMEM((2, rows, LANES), f32),
@@ -453,32 +537,29 @@
             collective_id=0, has_side_effects=True, vmem_limit_bytes=50 * 2**20
         ),
     )(
-        direction,
-        residual,
-        record_inverse,
-        precondition,
-        genetic_inverse,
-        sire_slot.reshape(rows, LANES),
-        dam_slot.reshape(rows, LANES),
-        sire_slot.reshape(1, animals),
-        dam_slot.reshape(1, animals),
-        send_rows.reshape(blocks, capacity),
-        genotyped_row.reshape(gen // LANES, LANES),
-        genotyped_row.reshape(1, gen),
-        allele_freq.reshape(1, markers),
-        marker_weight.reshape(1, markers),
-        genotypes,
+        hbm(direction),
+        hbm(residual),
+        hbm(record_inverse),
+        hbm(precondition),
+        hbm(genetic_inverse),
+        hbm(sire_slot.reshape(rows, LANES)),
+        hbm(dam_slot.reshape(rows, LANES)),
+        hbm(sire_slot.reshape(1, animals)),
+        hbm(dam_slot.reshape(1, animals)),
+        hbm(send_rows.reshape(blocks, capacity)),
+        hbm(genotyped_row.reshape(gen // LANES, LANES)),
+        hbm(genotyped_row.reshape(1, gen)),
+        hbm(allele_freq.reshape(1, markers)),
+        hbm(marker_weight.reshape(1, markers)),
+        hbm(genotypes),
+        hbm(solution),
     )
-    step = coef[0, 0]
-    ratio = coef[1, 0]
-    new_residual = residual - step * image
-    upper = precondition[0] * new_residual[0] + precondition[1] * new_residual[1]
-    lower = precondition[1] * new_residual[0] + precondition[2] * new_residual[1]
-    return (
-        solution + step * direction,
-        new_residual,
-        jnp.stack([upper, lower]) + ratio * direction,
-    )
+    return pl.pallas_call(
+        update,
+        out_shape=(jax.ShapeDtypeStruct((2, animals), f32),) * 3,
+        in_specs=[vmem] * 6,
+        out_specs=(vmem,) * 3,
+    )(*carried)
 
 
 def solution(mesh):

time: 50.8 us -> 45.5 us (0.90)
  local copies, waits for them, and re-layouts: 9.02 us -> 3.68 us
  Pallas kernels: 37.8 us -> 41 us
  other arithmetic: 2.61 us -> 0 us
    unnamed x26 -> x12, local copies, waits for them, and re-layouts: 8.48 us -> 3.68 us
    pallas_call x1 -> x2, Pallas kernels: 37.8 us -> 41 us  [the longest x1 39.2 us: on_device(): pl.pallas_call(functools.partial(kernel, blocks, layers), out_shape=(pair...]
    add x2 -> x0, other arithmetic: 2.03 us -> none  [the longest x1 1.93 us: on_device(): jnp.stack([upper, lower]) + ratio * direction]
    sub x1 -> x0, other arithmetic: 0.58 us -> none  [on_device(): new_residual = residual - step * image]
    slice x1 -> x0, local copies, waits for them, and re-layouts: 0.54 us -> none  [on_device(): ratio = coef[1, 0]]
where the time goes in v2:
time: 45.5 us; the launch traced here: 45.3 us
  Pallas kernels  41 us (90%)
  local copies, waits for them, and re-layouts  3.68 us (8%)
  between operations  0.66 us (1%)
    pallas_call x1, Pallas kernels, on_device(): pl.pallas_call(functools.partial(kernel, blocks, layers), out_shape=(pair...  39.2 us
    unnamed x12, local copies, waits for them, and re-layouts  3.68 us
    pallas_call x1, Pallas kernels, on_device(): pl.pallas_call(update, out_shape=(jax.ShapeDtypeStruct((2, animals), f32)...  1.77 us

profile of v2, /device:TPU:0, one launch (start us, length us, event | category | flops | bytes accessed | tf_op | source)
XLA Modules:
  0.0 45.3 jit_solution(7021094904216684417)
XLA Ops:
  0.6 39.2 %shard_map.148 = (f32[2,8192]{1,0:T(2,128)S(1)}, f32[2,128]{1,0:T(2,128)S(1)}, f32[2,8192]{1,0:T(2,128)S(1)}, f32[2,8192]{1,0:T(2,128)S(1)}, f32[3,8192]{1,0:T(4,128)S(1)}, /*index=5*/f32[2,8192]{1,0:T(2,128)S(1)}) custom-call(f32[2,8192]{1,0:T(2,128)} %direction_hbm.1, f32[2,8192]{1,0:T(2,128)} %residual_hbm.1, f32[3,8192]{1,0:T(4,128)} %record_inverse_hbm.1, ...), custom_call_target="tpu_custom_call" | custom-call | tf_op jit(solution)/shard_map/pallas_call | solution.py:486
  39.9 0.0 copy-start
  39.9 0.6 %copy-done = f32[3,8192]{1,0:T(4,128)} copy-done((f32[3,8192]{1,0:T(4,128)}, f32[3,8192]{1,0:T(4,128)S(1)}, u32[]{:S(2)}) %copy-start) | copy-done | bytes 98328
  40.5 0.0 copy-start.1
  40.5 0.6 %copy-done.1 = f32[2,8192]{1,0:T(2,128)} copy-done((f32[2,8192]{1,0:T(2,128)}, f32[2,8192]{1,0:T(2,128)S(1)}, u32[]{:S(2)}) %copy-start.1) | copy-done | bytes 65560
  41.1 0.0 copy-start.2
  41.1 0.6 %copy-done.2 = f32[2,8192]{1,0:T(2,128)} copy-done((f32[2,8192]{1,0:T(2,128)}, f32[2,8192]{1,0:T(2,128)S(1)}, u32[]{:S(2)}) %copy-start.2) | copy-done | bytes 65560
  41.8 0.0 copy-start.3
  41.8 0.6 %copy-done.3 = f32[2,8192]{1,0:T(2,128)} copy-done((f32[2,8192]{1,0:T(2,128)}, f32[2,8192]{1,0:T(2,128)S(1)}, u32[]{:S(2)}) %copy-start.3) | copy-done | bytes 65560
  42.4 0.0 copy-start.4
  42.4 0.6 %copy-done.4 = f32[2,8192]{1,0:T(2,128)} copy-done((f32[2,8192]{1,0:T(2,128)}, f32[2,8192]{1,0:T(2,128)S(1)}, u32[]{:S(2)}) %copy-start.4) | copy-done | bytes 65560
  43.0 0.0 copy-start.5
  43.0 0.5 %copy-done.5 = f32[2,128]{1,0:T(2,128)} copy-done((f32[2,128]{1,0:T(2,128)}, f32[2,128]{1,0:T(2,128)S(1)}, u32[]{:S(2)}) %copy-start.5) | copy-done | bytes 1048
  43.6 1.8 %shard_map.149 = (f32[2,8192]{1,0:T(2,128)}, f32[2,8192]{1,0:T(2,128)}, f32[2,8192]{1,0:T(2,128)}) custom-call(f32[2,8192]{1,0:T(2,128)} %copy-done.1, f32[2,128]{1,0:T(2,128)} %copy-done.5, f32[2,8192]{1,0:T(2,128)} %copy-done.2, f32[2,8192]{1,0:T(2,128)} %copy-done.3, f32[3,8192]{1,0:T(4,128)} %copy-done, f32[2,8192]{1,0:T(2,128)} %copy-done.4), custom_call_target="tpu_custom_call" | custom-call | tf_op jit(solution)/shard_map/pallas_call | solution.py:557
Async XLA Ops:
  39.9 0.6 %copy-start = (f32[3,8192]{1,0:T(4,128)}, f32[3,8192]{1,0:T(4,128)S(1)}, u32[]{:S(2)}) copy-start(f32[3,8192]{1,0:T(4,128)S(1)} %get-tuple-element.13.precondition) | copy-start | bytes 294916
  40.5 0.6 %copy-start.1 = (f32[2,8192]{1,0:T(2,128)}, f32[2,8192]{1,0:T(2,128)S(1)}, u32[]{:S(2)}) copy-start(f32[2,8192]{1,0:T(2,128)S(1)} %get-tuple-element.9.image) | copy-start | bytes 196612
  41.1 0.6 %copy-start.2 = (f32[2,8192]{1,0:T(2,128)}, f32[2,8192]{1,0:T(2,128)S(1)}, u32[]{:S(2)}) copy-start(f32[2,8192]{1,0:T(2,128)S(1)} %get-tuple-element.11.direction) | copy-start | bytes 196612
  41.8 0.6 %copy-start.3 = (f32[2,8192]{1,0:T(2,128)}, f32[2,8192]{1,0:T(2,128)S(1)}, u32[]{:S(2)}) copy-start(f32[2,8192]{1,0:T(2,128)S(1)} %get-tuple-element.12.residual) | copy-start | bytes 196612
  42.4 0.6 %copy-start.4 = (f32[2,8192]{1,0:T(2,128)}, f32[2,8192]{1,0:T(2,128)S(1)}, u32[]{:S(2)}) copy-start(f32[2,8192]{1,0:T(2,128)S(1)} %get-tuple-element.14.solution) | copy-start | bytes 196612
  43.0 0.5 %copy-start.5 = (f32[2,128]{1,0:T(2,128)}, f32[2,128]{1,0:T(2,128)S(1)}, u32[]{:S(2)}) copy-start(f32[2,128]{1,0:T(2,128)S(1)} %get-tuple-element.10.coef) | copy-start | bytes 3076

commit v3 on v2

--- a/solution.py
+++ b/solution.py
@@ -90,6 +90,7 @@
     ghosts,
     outbound,
     inbound,
+    parent,
     sampling,
     spread,
     gathered,
@@ -202,23 +203,17 @@
 
     wanted = [send_rows[:, k * LANES : (k + 1) * LANES] for k in range(spots)]
     wanted.append(picked_row[...])
-    wanted_high = [index >> 7 for index in wanted]
-    wanted_lane = [index & (LANES - 1) for index in wanted]
-
-    def pick_wanted(r, found):
-        out = []
-        for high, lane, (first, second) in zip(wanted_high, wanted_lane, found):
+    found = []
+    for index in wanted:
+        high, lane = index >> 7, index & (LANES - 1)
+        values = [jnp.zeros(index.shape, jnp.float32)] * 2
+        for r in range(rows):
             here = high == r
-            out.append(
-                (
-                    jnp.where(here, take(table[0, pl.ds(r, 1), :], lane, lane), first),
-                    jnp.where(here, take(table[1, pl.ds(r, 1), :], lane, lane), second),
-                )
-            )
-        return tuple(out)
-
-    zeros = tuple((jnp.zeros(i.shape, jnp.float32),) * 2 for i in wanted)
-    found = lax.fori_loop(0, rows, pick_wanted, zeros, unroll=4)
+            values = [
+                jnp.where(here, take(table[t, r : r + 1, :], lane, lane), values[t])
+                for t in range(2)
+            ]
+        found.append(values)
     for k in range(spots):
         for trait in range(2):
             for b in range(blocks):
@@ -270,44 +265,53 @@
     for load in loads[4:8]:
         load.wait()
     slots = [sire[...], dam[...]]
-    sums_of_parents = [jnp.zeros((rows, LANES), jnp.float32)] * 2
     known = (slots[0] >= 0).astype(jnp.float32) + (slots[1] >= 0).astype(jnp.float32)
-    parents = []
-    for slot in slots:
-        high = slot >> 7
-        lane = slot & (LANES - 1)
-
-        def local(r, carry, high=high, lane=lane):
-            here = high == r
-            return tuple(
-                jnp.where(here, take(table[t, pl.ds(r, 1), :], lane, lane), carry[t])
-                for t in range(2)
-            )
-
-        zero = jnp.zeros((rows, LANES), jnp.float32)
-        parents.append(lax.fori_loop(0, rows, local, (zero, zero), unroll=2))
+    group = 8
+
+    def local(i, carry):
+        at = pl.ds(pl.multiple_of(i * group, group), group)
+        for which, slot in enumerate((sire, dam)):
+            index = slot[at]
+            high, lane = index >> 7, index & (LANES - 1)
+            found = [jnp.zeros(index.shape, jnp.float32)] * 2
+            for r in range(rows):
+                here = high == r
+                found = [
+                    jnp.where(here, take(table[t, r : r + 1, :], lane, lane), found[t])
+                    for t in range(2)
+                ]
+            for t in range(2):
+                parent[which, t, at] = found[t]
+        return carry
+
+    lax.fori_loop(0, rows // group, local, 0)
     arrive("anim", blocks, me, ghosts, ghost_send, ghost_recv)
-    for which, slot in enumerate(slots):
-        high = slot >> 7
-        lane = slot & (LANES - 1)
-
-        def remote(source, carry, high=high, lane=lane):
-            for k in range(spots):
-                here = high == rows + source * spots + k
-                carry = tuple(
-                    jnp.where(
-                        here,
-                        take(ghosts[source, t * spots + k : t * spots + k + 1, :], lane, lane),
-                        carry[t],
-                    )
-                    for t in range(2)
-                )
-            return carry
-
-        parents[which] = lax.fori_loop(0, blocks, remote, parents[which])
+
+    def remote(i, carry):
+        at = pl.ds(pl.multiple_of(i * group, group), group)
+        for which, slot in enumerate((sire, dam)):
+            index = slot[at]
+            high, lane = index >> 7, index & (LANES - 1)
+            found = [parent[which, t, at] for t in range(2)]
+            for source in range(blocks):
+                for k in range(spots):
+                    here = high == rows + source * spots + k
+                    found = [
+                        jnp.where(
+                            here,
+                            take(ghosts[source, t * spots + k : t * spots + k + 1, :], lane, lane),
+                            found[t],
+                        )
+                        for t in range(2)
+                    ]
+            for t in range(2):
+                parent[which, t, at] = found[t]
+        return carry
+
+    lax.fori_loop(0, rows // group, remote, 0)
     factor = 1.0 / (1.0 - 0.25 * known)
     for t in range(2):
-        sampling[t] = factor * (table[t] - 0.5 * (parents[0][t] + parents[1][t]))
+        sampling[t] = factor * (table[t] - 0.5 * (parent[0, t] + parent[1, t]))
 
     spread[...] = jnp.zeros(spread.shape, jnp.float32)
     lines_per_step = STEP // LANES
@@ -515,6 +519,7 @@
             pltpu.VMEM(lists, f32),
             pltpu.VMEM(lists, f32),
             pltpu.VMEM(lists, f32),
+            pltpu.VMEM((2, 2, rows, LANES), f32),
             pltpu.VMEM((2, rows, LANES), f32),
             pltpu.VMEM((4 * full_high, WIDE), f32),
             pltpu.VMEM((2, animals // WIDE, WIDE), f32),
@@ -559,7 +564,8 @@
         out_shape=(jax.ShapeDtypeStruct((2, animals), f32),) * 3,
         in_specs=[vmem] * 6,
         out_specs=(vmem,) * 3,
-    )(*carried)
+        compiler_params=pltpu.CompilerParams(vmem_limit_bytes=8 * 2**20),
+    )(*[pltpu.with_memory_space_constraint(value, pltpu.VMEM) for value in carried])
 
 
 def solution(mesh):

time: 45.5 us -> 30.6 us (0.67)
  Pallas kernels: 41 us -> 29.8 us
  local copies, waits for them, and re-layouts: 3.68 us -> 0 us
    pallas_call x1, Pallas kernels: 39.2 us -> 29.1 us  [on_device(): pl.pallas_call(functools.partial(kernel, blocks, layers), out_shape=(pair...]
    unnamed x12 -> x0, local copies, waits for them, and re-layouts: 3.68 us -> none
    pallas_call x1, Pallas kernels: 1.77 us -> 0.76 us  [on_device(): pl.pallas_call(update, out_shape=(jax.ShapeDtypeStruct((2, animals), f32)...]
where the time goes in v3:
time: 30.6 us; the launch traced here: 30.5 us
  Pallas kernels  29.8 us (97%)
  between operations  0.64 us (2%)
    pallas_call x1, Pallas kernels, on_device(): pl.pallas_call(functools.partial(kernel, blocks, layers), out_shape=(pair...  29.1 us
    pallas_call x1, Pallas kernels, on_device(): pl.pallas_call(update, out_shape=(jax.ShapeDtypeStruct((2, animals), f32)...  0.76 us

profile of v3, /device:TPU:0, one launch (start us, length us, event | category | flops | bytes accessed | tf_op | source)
XLA Modules:
  0.0 30.5 jit_solution(3418955949626825425)
XLA Ops:
  0.6 29.1 %shard_map.148 = (f32[2,8192]{1,0:T(2,128)S(1)}, f32[2,128]{1,0:T(2,128)S(1)}, f32[2,8192]{1,0:T(2,128)S(1)}, f32[2,8192]{1,0:T(2,128)S(1)}, f32[3,8192]{1,0:T(4,128)S(1)}, /*index=5*/f32[2,8192]{1,0:T(2,128)S(1)}) custom-call(f32[2,8192]{1,0:T(2,128)} %direction_hbm.1, f32[2,8192]{1,0:T(2,128)} %residual_hbm.1, f32[3,8192]{1,0:T(4,128)} %record_inverse_hbm.1, ...), custom_call_target="tpu_custom_call" | custom-call | tf_op jit(solution)/shard_map/pallas_call | solution.py:490
  29.7 0.8 %shard_map.149 = (f32[2,8192]{1,0:T(2,128)}, f32[2,8192]{1,0:T(2,128)}, f32[2,8192]{1,0:T(2,128)}) custom-call(f32[2,8192]{1,0:T(2,128)S(1)} %get-tuple-element.9.image, f32[2,128]{1,0:T(2,128)S(1)} %get-tuple-element.10.coef, f32[2,8192]{1,0:T(2,128)S(1)} %get-tuple-element.11.direction, f32[2,8192]{1,0:T(2,128)S(1)} %get-tuple-element.12.residual, ...), custom_call_target="tpu_custom_call" | custom-call | tf_op jit(solution)/shard_map/pallas_call | solution.py:562

commit v4 on v3

--- a/solution.py
+++ b/solution.py
@@ -9,7 +9,7 @@
 
 LANES = 128
 WIDE = 256
-STEP = 512
+STEP = 2048
 MESH = pl.DeviceIdType.MESH
 
 

time: 30.6 us -> 27.4 us (0.90)
  Pallas kernels: 29.8 us -> 26.6 us
    pallas_call x1, Pallas kernels: 29.1 us -> 25.8 us  [on_device(): pl.pallas_call(functools.partial(kernel, blocks, layers), out_shape=(pair...]
where the time goes in v4:
time: 27.4 us; the launch traced here: 27.2 us
  Pallas kernels  26.6 us (97%)
  between operations  0.64 us (2%)
    pallas_call x1, Pallas kernels, on_device(): pl.pallas_call(functools.partial(kernel, blocks, layers), out_shape=(pair...  25.8 us
    pallas_call x1, Pallas kernels, on_device(): pl.pallas_call(update, out_shape=(jax.ShapeDtypeStruct((2, animals), f32)...  0.75 us

profile of v4, /device:TPU:0, one launch (start us, length us, event | category | flops | bytes accessed | tf_op | source)
XLA Modules:
  0.0 27.2 jit_solution(8136781137205343658)
XLA Ops:
  0.6 25.8 %shard_map.148 = (f32[2,8192]{1,0:T(2,128)S(1)}, f32[2,128]{1,0:T(2,128)S(1)}, f32[2,8192]{1,0:T(2,128)S(1)}, f32[2,8192]{1,0:T(2,128)S(1)}, f32[3,8192]{1,0:T(4,128)S(1)}, /*index=5*/f32[2,8192]{1,0:T(2,128)S(1)}) custom-call(f32[2,8192]{1,0:T(2,128)} %direction_hbm.1, f32[2,8192]{1,0:T(2,128)} %residual_hbm.1, f32[3,8192]{1,0:T(4,128)} %record_inverse_hbm.1, ...), custom_call_target="tpu_custom_call" | custom-call | tf_op jit(solution)/shard_map/pallas_call | solution.py:490
  26.5 0.7 %shard_map.149 = (f32[2,8192]{1,0:T(2,128)}, f32[2,8192]{1,0:T(2,128)}, f32[2,8192]{1,0:T(2,128)}) custom-call(f32[2,8192]{1,0:T(2,128)S(1)} %get-tuple-element.9.image, f32[2,128]{1,0:T(2,128)S(1)} %get-tuple-element.10.coef, f32[2,8192]{1,0:T(2,128)S(1)} %get-tuple-element.11.direction, f32[2,8192]{1,0:T(2,128)S(1)} %get-tuple-element.12.residual, ...), custom_call_target="tpu_custom_call" | custom-call | tf_op jit(solution)/shard_map/pallas_call | solution.py:562
